TPU v7x, 32 devices: a whole 2x2x4 slice. The times are simulated.
32 devices in a mesh: tm: 8 (over z, y), elec: 4 (over x, core).
Axes of the slice: x: 2, y: 2, z: 4, core: 2. Of those that a mesh axis runs over, the one named last changes fastest.
Arguments:
- signal: bfloat16 [16, 1024, 256], P('elec', 'tm'), may hold values from -16 to 16
- w_qkv: bfloat16 [256, 1152], replicated, may hold values from -0.375 to 0.375
- w_decay: bfloat16 [256, 4], replicated, may hold values from -0.375 to 0.375
- decay_rate: float32 [4], replicated, may hold values from 0.00048828125 to 0.05
- lin_gain: float32 [128], replicated, may hold values from 0.25 to 1.75
- w_out: bfloat16 [384, 256], replicated, may hold values from -0.3125 to 0.3125
- valid: int32 [16], replicated, may hold values 0 or 1
- boundary: int32 [1024], P('tm'), may hold values 0 or 1
Outputs:
- encoded: bfloat16 [16, 1024, 256], P('elec', 'tm')
All inputs are finite; a program needn't handle non-finite values. No bound on the sum of `boundary` on one device may be relied on, other than what follows from the above.
Results may differ from a plain program's by a relative error of at most 0.006.
The roundings to bfloat16 on the way count: a program that leaves them out, or rounds other values in their place, can miss the bound.
Values may be sent and summed in bfloat16 or wider, within the bound.
A program may use at most 128 MiB of HBM per device.

v0:
```python
import math

import jax
import jax.numpy as jnp
from jax import lax
from jax.sharding import PartitionSpec as P

WIN = 128


def prefix(shard, axis, join, neutral):
    place = lax.axis_index(axis)
    gathered = jax.tree.map(
        lambda a, kind: lax.all_gather(a.astype(kind), axis), shard, (jnp.bfloat16, jnp.bfloat16)
    )
    state = jax.tree.map(lambda a, e: jnp.zeros_like(a) + jnp.asarray(e, a.dtype), shard, neutral)

    def one(turn, state):
        return join(
            state,
            jax.tree.map(
                lambda a, own: lax.dynamic_index_in_dim(a, turn, 0, False).astype(own.dtype),
                gathered,
                shard,
            ),
        )

    return lax.fori_loop(0, place, one, state)


def passed_along(value, axis, steps):
    count = lax.axis_size(axis)
    first, last = (max(0, -steps), min(count, count - steps))
    return lax.ppermute(value, axis, [(source, source + steps) for source in range(first, last)])


def linear_local(query, keys, payload_entries, log_decay):
    head_dim = query.shape[-1]
    step_count = query.shape[1]
    cumulative = jnp.cumsum(log_decay, axis=1)
    by_head = jnp.transpose(cumulative, (0, 2, 1))
    spread = by_head[:, :, :, None] - by_head[:, :, None, :]
    positions = jnp.arange(step_count, dtype=jnp.int32)
    causal = positions[:, None] >= positions[None, :]
    decays = jnp.where(causal, jnp.exp(jnp.where(causal, spread, 0.0)), 0.0)
    scores = jnp.einsum(
        "ethd,eshd->ehts", query, keys, preferred_element_type=jnp.float32
    ) * head_dim ** (-0.5)
    weights = (scores * decays).astype(jnp.bfloat16)
    intra = jnp.einsum(
        "ehts,eshd->ethd", weights, payload_entries, preferred_element_type=jnp.float32
    )
    ending = cumulative[:, -1, :]
    kept = jnp.exp(ending[:, None, :] - cumulative)
    local_state = jnp.einsum(
        "eshd,eshf->ehdf",
        keys.astype(jnp.float32) * kept[..., None],
        payload_entries.astype(jnp.float32),
        precision=lax.Precision.HIGHEST,
    )
    return (intra, cumulative, jnp.exp(ending), local_state)


def carried_in(query, cumulative, state):
    head_dim = query.shape[-1]
    lifted = query.astype(jnp.float32) * (jnp.exp(cumulative) * head_dim ** (-0.5))[..., None]
    return jnp.einsum("ethd,ehdf->ethf", lifted, state, precision=lax.Precision.HIGHEST)


def window_attend(query, keys, payload_entries, query_start, key_start):
    elec_count, row_count, head_count, head_dim = query.shape
    key_count = keys.shape[1]
    query_pos = query_start + jnp.arange(row_count, dtype=jnp.int32)
    key_pos = key_start + jnp.arange(key_count, dtype=jnp.int32)
    allowed = (
        (key_pos[None, :] <= query_pos[:, None])
        & (key_pos[None, :] >= query_pos[:, None] - WIN)
        & (key_pos[None, :] >= 0)
    )
    allowed = allowed[None, None]
    scores = jnp.einsum(
        "ethd,eshd->ehts", query, keys, preferred_element_type=jnp.float32
    ) * head_dim ** (-0.5)
    masked = jnp.where(allowed, scores, -jnp.inf)
    row_peak = jnp.max(masked, axis=-1)
    expweights = jnp.exp(jnp.where(allowed, scores - row_peak[..., None], -jnp.inf))
    totals = jnp.sum(expweights, axis=-1)
    rounded = expweights.astype(jnp.bfloat16)
    summed = jnp.einsum(
        "ehts,eshd->ethd", rounded, payload_entries, preferred_element_type=jnp.float32
    )
    outputs = summed / jnp.transpose(totals, (0, 2, 1))[..., None]
    return outputs.reshape(elec_count, row_count, head_count * head_dim)


def shards(signal, w_qkv, w_decay, decay_rate, lin_gain, w_out, valid, boundary):
    elec_rows, time_rows, model_width = signal.shape
    head_count = decay_rate.shape[0]
    inner_width = lin_gain.shape[0]
    head_dim = inner_width // head_count
    flat_rows = signal.reshape(elec_rows * time_rows, model_width)
    projected = jnp.dot(flat_rows, w_qkv, preferred_element_type=jnp.float32).astype(jnp.bfloat16)
    projected = projected.reshape(elec_rows, time_rows, 9, inner_width)
    logits = jnp.dot(flat_rows, w_decay, preferred_element_type=jnp.float32).reshape(
        elec_rows, time_rows, head_count
    )
    log_decay = -2.0 * decay_rate * jax.nn.sigmoid(logits) + boundary[None, :, None].astype(
        jnp.float32
    ) * math.log(0.5)
    shape_four = (elec_rows, time_rows, head_count, head_dim)
    lin_query = projected[:, :, 0].reshape(shape_four)
    intra, cumulative, decay_all, local_state = linear_local(
        lin_query,
        projected[:, :, 1].reshape(shape_four),
        projected[:, :, 2].reshape(shape_four),
        log_decay,
    )

    def chain(earlier, later):
        return (earlier[0] * later[0], later[0][..., None, None] * earlier[1] + later[1])

    identity = (jnp.ones_like(decay_all), jnp.zeros_like(local_state))
    entering = prefix((decay_all, local_state), "tm", chain, identity)
    lin_raw = (intra + carried_in(lin_query, cumulative, entering[1])).reshape(
        elec_rows, time_rows, inner_width
    )
    mean_square = jnp.mean(lin_raw * lin_raw, axis=-1, keepdims=True)
    lin_out = lin_raw * lax.rsqrt(mean_square + 1e-05) * lin_gain
    win_keys = projected[:, :, 4]
    win_values = projected[:, :, 5]
    prior_keys, prior_values = passed_along((win_keys, win_values), "tm", 1)
    all_keys = jnp.concatenate([prior_keys, win_keys], axis=1).reshape(
        elec_rows, time_rows + WIN, head_count, head_dim
    )
    all_values = jnp.concatenate([prior_values, win_values], axis=1).reshape(
        elec_rows, time_rows + WIN, head_count, head_dim
    )
    query_start = lax.axis_index("tm") * time_rows
    win_out = window_attend(
        projected[:, :, 3].reshape(shape_four), all_keys, all_values, query_start, query_start - WIN
    )
    ele_query = projected[:, :, 6]
    ele_keys = projected[:, :, 7]
    ele_values = projected[:, :, 8]
    query_four = ele_query.reshape(shape_four)
    own_rows = lax.axis_index("elec") * elec_rows + jnp.arange(elec_rows, dtype=jnp.int32)
    start_peak = jnp.full((head_count, elec_rows, time_rows), -1e30, jnp.float32)
    piece_keys = lax.all_gather(ele_keys, "elec", axis=0, tiled=True)
    piece_values = lax.all_gather(ele_values, "elec", axis=0, tiled=True)
    piece_count = piece_keys.shape[0]
    keys_four = piece_keys.reshape(piece_count, time_rows, head_count, head_dim)
    values_four = piece_values.reshape(piece_count, time_rows, head_count, head_dim)
    scores = jnp.einsum(
        "ethd,jthd->hejt", query_four, keys_four, preferred_element_type=jnp.float32
    ) * head_dim ** (-0.5)
    columns = jnp.arange(piece_count, dtype=jnp.int32)
    piece_valid = valid == 1
    allowed = (piece_valid[None, :] | (own_rows[:, None] == columns[None, :]))[None, :, :, None]
    masked = jnp.where(allowed, scores, -jnp.inf)
    new_peak = jnp.maximum(start_peak, jnp.max(masked, axis=2))
    expweights = jnp.exp(jnp.where(allowed, scores - new_peak[:, :, None, :], -jnp.inf))
    new_totals = jnp.sum(expweights, axis=2)
    new_accum = jnp.einsum(
        "hejt,jthd->hedt",
        expweights.astype(jnp.bfloat16),
        values_four,
        preferred_element_type=jnp.float32,
    )
    mixed_heads = new_accum / new_totals[:, :, None, :]
    ele_out = (
        jnp.transpose(mixed_heads, (1, 3, 0, 2))
        .reshape(elec_rows, time_rows, inner_width)
        .astype(jnp.bfloat16)
    )
    mixed = jnp.concatenate(
        [lin_out.astype(jnp.bfloat16), win_out.astype(jnp.bfloat16), ele_out], axis=-1
    )
    update = jnp.dot(
        mixed.reshape(elec_rows * time_rows, 3 * inner_width),
        w_out,
        preferred_element_type=jnp.float32,
    )
    encoded = (flat_rows.astype(jnp.float32) + update).astype(jnp.bfloat16)
    return encoded.reshape(elec_rows, time_rows, model_width)


def solution(mesh):
    return jax.shard_map(
        shards,
        mesh=mesh,
        in_specs=(P("elec", "tm", None), P(), P(), P(), P(), P(), P(), P("tm")),
        out_specs=P("elec", "tm", None),
        check_vma=False,
    )
```

profile of v0, /device:TPU:0, one launch (start us, length us, event | category | flops | bytes accessed | tf_op | source)
XLA Modules:
  0.0 119.2 jit_solution(12134720386130571115)
XLA Ops:
  0.0 0.0 copy-start
  0.0 1.1 copy-done
  1.1 1.5 %convolution_convert_fusion = bf16[512,1152]{1,0:T(8,128)(2,1)S(1)} fusion(bf16[512,256]{1,0:T(8,128)(2,1)} %bitcast.107, bf16[256,1152]{1,0:T(8,128)(2,1)S(1)} %copy-done), kind=kOutput, calls=%fused_computation.3 | convolution fusion | flops 302579712 | bytes 2031616 | tf_op jit(solution)/shard_map/dot_general | solution.py:102
  2.5 0.6 copy.114
  3.1 0.3 reshape.229
  3.5 0.0 copy-start.8
  3.5 0.0 copy-start.9
  3.5 0.0 copy-start.3
  3.5 0.0 copy-start.7
  3.5 1.2 fusion.79
  4.7 0.8 copy.131
  5.5 5.5 %collective-permute-start.1 = (bf16[4,128,128]{2,1,0:T(8,128)(2,1)}, bf16[4,128,128]{2,1,0:T(8,128)(2,1)}, u32[]{:S(2)}, u32[]{:S(2)}) collective-permute-start(bf16[4,128,128]{2,1,0:T(8,128)(2,1)} %bitcast.16), channel_id=1, source_target_pairs={{0,4},{4,8},{8,12},{12,16},{16,20},{20,24},{24,28},{1,5},{5,9},{9,... | collective-permute-start | bytes 393224 | tf_op jit(solution)/shard_map/ppermute | solution.py:34
  11.0 0.8 copy.127
  11.7 3.4 %collective-permute-start = (bf16[4,128,128]{2,1,0:T(8,128)(2,1)}, bf16[4,128,128]{2,1,0:T(8,128)(2,1)}, u32[]{:S(2)}, u32[]{:S(2)}) collective-permute-start(bf16[4,128,128]{2,1,0:T(8,128)(2,1)} %bitcast.12), channel_id=1, source_target_pairs={{0,4},{4,8},{8,12},{12,16},{16,20},{20,24},{24,28},{1,5},{5,9},{9,... | collective-permute-start | bytes 393224 | tf_op jit(solution)/shard_map/ppermute | solution.py:34
  15.2 0.7 copy.133
  15.9 0.7 copy.129
  16.6 0.0 copy-done.8
  16.6 0.0 copy-done.9
  16.6 0.0 copy-done.3
  16.7 0.2 fusion.18
  16.9 0.2 copy.118
  17.0 0.3 reduce_window_sum.11
  17.3 0.1 exponential_multiply_fusion
  17.4 0.1 copy.122
  17.5 0.3 convolution_convert_fusion.1
  17.8 32.9 %all-gather.1 = bf16[32,4,32,32]{3,2,1,0:T(8,128)(2,1)S(1)} all-gather(bf16[4,4,32,32]{3,2,1,0:T(8,128)(2,1)S(1)} %convolution_convert_fusion.1), channel_id=3, replica_groups=mesh['tm'=8,'elec'=4] {'tm'}, dimensions={0}, use_global_device_ids=true | all-gather | bytes 294912 | tf_op jit(solution)/shard_map/all_gather | solution.py:14
  50.8 26.0 %all-gather = bf16[32,1,4]{2,1,0:T(2,128)(2,1)S(1)} all-gather(bf16[4,1,4]{2,1,0:T(2,128)(2,1)S(1)} %get-tuple-element.97), channel_id=2, replica_groups=mesh['tm'=8,'elec'=4] {'tm'}, dimensions={0}, use_global_device_ids=true | all-gather | bytes 288 | tf_op jit(solution)/shard_map/all_gather | solution.py:14
  76.8 0.1 copy.124
  76.9 0.1 copy.119
  77.0 0.6 fusion.54
  77.7 0.8 multiply_reduce_fusion
  78.4 0.2 copy.126
  78.6 0.7 copy.130
  79.3 0.1 copy.137
  79.4 7.2 %all-gather.3 = bf16[16,128,1,128]{3,1,2,0:T(8,128)(2,1)S(1)} all-gather(bf16[4,128,1,128]{3,1,2,0:T(8,128)(2,1)S(1)} %copy.137), channel_id=5, replica_groups=mesh['tm'=8,'elec'=4] {'elec'}, dimensions={0}, use_global_device_ids=true | all-gather | bytes 655360 | tf_op jit(solution)/shard_map/all_gather | solution.py:148
  86.6 0.3 copy.138
  86.9 1.6 %copy.140 = bf16[16,128,4,32]{3,0,1,2:T(8,128)(2,1)S(1)} copy(bf16[16,128,4,32]{1,3,2,0:T(8,128)(2,1)S(1)} %bitcast.91) | data formatting | bytes 1048576 | tf_op jit(solution)/shard_map/reshape | solution.py:151
  88.5 1.3 %copy.141 = bf16[4,128,4,32]{3,0,1,2:T(4,128)(2,1)S(1)} copy(bf16[4,128,4,32]{1,0,3,2:T(4,128)(2,1)} %bitcast.95) | data formatting | bytes 262144 | tf_op jit(solution)/shard_map/reshape;squeeze | solution.py:145
  89.9 0.1 fusion.66
  90.0 2.2 %select_reduce_fusion.1 = (f32[4,4,128]{1,2,0:T(8,128)S(1)}, f32[4,4,16,128]{2,1,3,0:T(4,128)}) fusion(pred[4,16]{1,0:T(4,128)(4,1)S(1)} %fusion.66, bf16[16,128,4,32]{3,0,1,2:T(8,128)(2,1)S(1)} %copy.140, bf16[4,128,4,32]{3,0,1,2:T(4,128)(2,1)S(1)} %copy.141), kind=kOutput, calls=%fused_computation.29 | convolution fusion | flops 2193408 | bytes 794688 | tf_op jit(solution)/shard_map/ethd,jthd->hejt/dot_general | solution.py:153
  92.2 0.7 broadcast_maximum_fusion
  92.9 1.0 copy.135
  93.9 7.5 %all-gather.2 = bf16[16,128,1,128]{3,1,2,0:T(8,128)(2,1)S(1)} all-gather(bf16[4,128,1,128]{3,1,2,0:T(8,128)(2,1)S(1)} %copy.135), channel_id=4, replica_groups=mesh['tm'=8,'elec'=4] {'elec'}, dimensions={0}, use_global_device_ids=true | all-gather | bytes 655360 | tf_op jit(solution)/shard_map/all_gather | solution.py:149
  101.4 0.3 copy.136
  101.7 1.6 %copy.142 = bf16[16,128,4,32]{3,0,1,2:T(8,128)(2,1)S(1)} copy(bf16[16,128,4,32]{1,3,2,0:T(8,128)(2,1)S(1)} %bitcast.92) | data formatting | bytes 1048576 | tf_op jit(solution)/shard_map/reshape | solution.py:152
  103.3 2.4 %fusion.27 = f32[4,4,128]{1,2,0:T(8,128)S(1)} fusion(f32[4,4,16,128]{2,1,3,0:T(4,128)} %get-tuple-element.99, f32[4,4,128]{1,2,0:T(8,128)} %broadcast_maximum_fusion, pred[4,16]{1,0:T(4,128)(4,1)S(1)} %fusion.66), kind=kLoop, calls=%fused_computation.38 | loop fusion | flops 96256 | bytes 147520 | tf_op jit(solution)/shard_map/reduce_sum | solution.py:162
  105.7 3.2 %fusion.29 = f32[4,128,32,4]{2,3,1,0:T(4,128)} fusion(bf16[16,128,4,32]{3,0,1,2:T(8,128)(2,1)S(1)} %copy.142, f32[4,4,16,128]{2,1,3,0:T(4,128)} %get-tuple-element.99, f32[4,4,128]{1,2,0:T(8,128)} %broadcast_maximum_fusion, pred[4,16]{1,0:T(4,128)(4,1)S(1)} %fusion.66), kind=kOutput, calls=%fused_computation.40 | convolution fusion | flops 2195456 | bytes 925760 | tf_op jit(solution)/shard_map/hejt,jthd->hedt/dot_general | solution.py:163
  108.9 1.6 %copy.143 = f32[4,128,32,4]{1,2,0,3:T(8,128)S(1)} copy(f32[4,128,32,4]{2,3,1,0:T(4,128)} %fusion.29) | data formatting | bytes 524288 | tf_op jit(solution)/shard_map/hejt,jthd->hedt/dot_general | solution.py:163
  110.5 0.1 copy.144
  110.6 0.1 copy.145
  110.8 0.1 fusion.45
  110.9 0.1 and_and_fusion
  111.0 0.0 collective-permute-done.1
  111.0 1.0 copy.132
  112.0 0.0 copy-done.1
  112.0 0.0 copy-done.2
  112.0 0.5 fusion.49
  112.5 1.1 fusion.81
  113.7 0.0 collective-permute-done
  113.7 1.0 copy.128
  114.7 0.0 copy-start.4
  114.7 1.5 %fusion.13 = bf16[4,128,4,32]{1,3,2,0:T(8,128)(2,1)} fusion(bf16[4,128,4,32]{1,3,2,0:T(8,128)(2,1)S(1)} %bitcast.109, bf16[4,128,4,32]{1,3,2,0:T(8,128)(2,1)S(1)} %bitcast.111, f32[4,4,128,256]{3,2,1,0:T(8,128)S(1)} %fusion.49, pred[128,256]{1,0:T(8,128)(4,1)S(1)} %and_and_fusion, f32[4,128,4]{1,2,0:T(4,128)S(1)} %bitcast.115), kind=kOutput, calls=%fused_computation.21 | convolution fusion | flops 37357824 | bytes 2531328 | tf_op jit(solution)/shard_map/ehts,eshd->ethd/dot_general | solution.py:89
  116.2 1.0 copy.134
  117.3 2.0 %fusion.9 = bf16[512,256]{1,0:T(8,128)(2,1)} fusion(bf16[384,256]{1,0:T(8,128)(2,1)} %param.15, bf16[512,256]{1,0:T(8,128)(2,1)S(1)} %bitcast.108, bf16[512,128]{0,1:T(8,128)(2,1)S(1)} %bitcast.110, bf16[512,128]{0,1:T(8,128)(2,1)S(1)} %bitcast.112, bf16[512,128]{0,1:T(8,128)(2,1)S(1)} %fusion.45), kind=kOutput, calls=%fused_computation.15 | convolution fusion | flops 102236160 | bytes 1114112 | tf_op jit(solution)/shard_map/dot_general | solution.py:178
  (29 shorter events, 0.3 us)
Async XLA Ops:
  0.0 1.1 copy-start
  3.5 13.1 %copy-start.8 = (f32[4]{0:T(128)S(1)}, f32[4]{0:T(128)}, u32[]{:S(2)}) copy-start(f32[4]{0:T(128)} %param.13) | copy-start | bytes 52
  3.5 13.1 %copy-start.9 = (s32[128]{0:T(128)S(1)}, s32[128]{0:T(128)}, u32[]{:S(2)}) copy-start(s32[128]{0:T(128)} %param.17) | copy-start | bytes 1540
  3.5 13.1 %copy-start.3 = (bf16[4,128,256]{2,1,0:T(8,128)(2,1)S(1)}, bf16[4,128,256]{2,1,0:T(8,128)(2,1)}, u32[]{:S(2)}) copy-start(bf16[4,128,256]{2,1,0:T(8,128)(2,1)} %param.10) | copy-start | bytes 786436
  3.5 13.1 %copy-start.7 = (bf16[256,4]{0,1:T(4,128)(2,1)S(1)}, bf16[256,4]{0,1:T(4,128)(2,1)}, u32[]{:S(2)}) copy-start(bf16[256,4]{0,1:T(4,128)(2,1)} %param.12) | copy-start | bytes 6148
  5.5 105.5 %collective-permute-start.1 = (bf16[4,128,128]{2,1,0:T(8,128)(2,1)}, bf16[4,128,128]{2,1,0:T(8,128)(2,1)}, u32[]{:S(2)}, u32[]{:S(2)}) collective-permute-start(bf16[4,128,128]{2,1,0:T(8,128)(2,1)} %bitcast.16), channel_id=1, source_target_pairs={{0,4},{4,8},{8,12},{12,16},{16,20},{20,24},{24,28},{1,5},{5,9},{9,... | collective-permute-start | bytes 393224 | tf_op jit(solution)/shard_map/ppermute | solution.py:34
  11.7 101.9 %collective-permute-start = (bf16[4,128,128]{2,1,0:T(8,128)(2,1)}, bf16[4,128,128]{2,1,0:T(8,128)(2,1)}, u32[]{:S(2)}, u32[]{:S(2)}) collective-permute-start(bf16[4,128,128]{2,1,0:T(8,128)(2,1)} %bitcast.12), channel_id=1, source_target_pairs={{0,4},{4,8},{8,12},{12,16},{16,20},{20,24},{24,28},{1,5},{5,9},{9,... | collective-permute-start | bytes 393224 | tf_op jit(solution)/shard_map/ppermute | solution.py:34
  86.6 3.3 %copy-start.10 = (s32[16]{0:T(128)S(1)}, s32[16]{0:T(128)}, u32[]{:S(2)}) copy-start(s32[16]{0:T(128)} %param.16) | copy-start | bytes 196
  108.9 1.9 %copy-start.6 = (f32[128]{0:T(128)S(1)}, f32[128]{0:T(128)}, u32[]{:S(2)}) copy-start(f32[128]{0:T(128)} %param.14) | copy-start | bytes 1540
  108.9 3.1 %copy-start.1 = (bf16[4,128,1,128]{1,3,0,2:T(8,128)(2,1)S(1)}, bf16[4,128,1,128]{1,3,0,2:T(8,128)(2,1)}, u32[]{:S(2)}) copy-start(bf16[4,128,1,128]{1,3,0,2:T(8,128)(2,1)} %copy.133) | copy-start | bytes 393220
  108.9 3.1 %copy-start.2 = (bf16[4,128,1,128]{1,3,0,2:T(8,128)(2,1)S(1)}, bf16[4,128,1,128]{1,3,0,2:T(8,128)(2,1)}, u32[]{:S(2)}) copy-start(bf16[4,128,1,128]{1,3,0,2:T(8,128)(2,1)} %copy.130) | copy-start | bytes 393220
  112.5 2.2 %copy-start.5 = (bf16[4,128,1,128]{1,3,0,2:T(8,128)(2,1)S(1)}, bf16[4,128,1,128]{1,3,0,2:T(8,128)(2,1)}, u32[]{:S(2)}) copy-start(bf16[4,128,1,128]{1,3,0,2:T(8,128)(2,1)} %copy.129) | copy-start | bytes 393220
  114.7 2.6 %copy-start.4 = (bf16[4,128,256]{2,1,0:T(8,128)(2,1)S(1)}, bf16[4,128,256]{2,1,0:T(8,128)(2,1)}, u32[]{:S(2)}) copy-start(bf16[4,128,256]{2,1,0:T(8,128)(2,1)} %param.10) | copy-start | bytes 786436
where the time goes:
time: 120 us; the launch traced here: 119 us
  blocking collectives  73.5 us (61%)
  local copies, waits for them, and re-layouts  18.7 us (16%)
  matrix products  12.7 us (11%)
  starting transfers between devices  8.94 us (7%)
  other arithmetic  4.92 us (4%)
    all_gather x2, blocking collectives, prefix(): lax.all_gather(a.astype(kind), axis)  58.9 us
    ppermute x2, starting transfers between devices, passed_along(): lax.ppermute(value, axis, [(source, source + steps) for source in range(f...  8.94 us
    all_gather x1, blocking collectives, shards(): piece_values = lax.all_gather(ele_values, 'elec', axis=0, tiled=True)  7.47 us
    all_gather x1, blocking collectives, shards(): piece_keys = lax.all_gather(ele_keys, 'elec', axis=0, tiled=True)  7.16 us
    dot_general x1, matrix products, shards(): jnp.einsum('hejt,jthd->hedt', expweights.astype(jnp.bfloat16), values_fou...  3.16 us
  transfers between devices with their start and end apart: 2, of which 0 were waited for; matrix products, arithmetic and copies ran while one was open for 21% of the time, Pallas kernels for 0%

commit v1 on v0

v1 whole, which is shorter than its diff:
```python
import functools
import math

import jax
import jax.numpy as jnp
from jax import lax
from jax.experimental import pallas as pl
from jax.experimental.pallas import tpu as pltpu
from jax.sharding import PartitionSpec as P

WIN = 128
HEADS = 4
INNER = 128
LOG2E = 1.0 / math.log(2.0)
F32 = jnp.float32
BF16 = jnp.bfloat16
MESH = pl.DeviceIdType.MESH
GROUP = 8


def dot(a, b):
    return jnp.dot(a, b, preferred_element_type=F32)


def dot_t(a, b):
    return lax.dot_general(a, b, (((1,), (1,)), ((), ())), preferred_element_type=F32)


def split(a):
    high = a.astype(BF16)
    return high, (a - high.astype(F32)).astype(BF16)


def iota(shape, dim):
    return lax.broadcasted_iota(jnp.int32, shape, dim)


def kernel(
    n_tm,
    chunks,
    sig_in,
    wqkv_in,
    wdec_ref,
    rate_ref,
    gain_ref,
    wout_in,
    valid_ref,
    bound_ref,
    out_ref,
    sig,
    wqkv,
    wout,
    wd,
    esig,
    wsig,
    proj,
    ekv,
    eq,
    cum_lanes,
    raw,
    ele,
    msg,
    got,
    local_sem,
    esend,
    erecv,
    wsend,
    wrecv,
    ssend,
    srecv,
):
    elecs, times, width = sig.shape
    hd = INNER // HEADS
    scale = hd**-0.5
    me = lax.axis_index("tm")
    who = lax.axis_index("elec")
    sib = who + 1 - 2 * lax.rem(who, 2)
    far = lax.rem(who + 2, 4)
    far_sib = lax.rem(sib + 2, 4)
    rounds = []
    step = 1
    while step < n_tm:
        rounds.append(step)
        step *= 2
    per = times // chunks

    local = [
        pltpu.make_async_copy(src, dst, local_sem.at[i])
        for i, (src, dst) in enumerate(((sig_in, sig), (wqkv_in, wqkv), (wout_in, wout)))
    ]
    for copy in local:
        copy.start()
    barrier = pltpu.get_barrier_semaphore()
    for peer in (sib, far):
        pl.semaphore_signal(barrier, inc=1, device_id={"elec": peer}, device_id_type=MESH)
    targets = 2
    for d in rounds:
        targets = targets + jnp.where(me + d < n_tm, 1, 0)

        @pl.when(me >= d)
        def _():
            pl.semaphore_signal(barrier, inc=1, device_id={"tm": me - d}, device_id_type=MESH)

    @pl.when(me == 0)
    def _():
        wsig[...] = jnp.zeros_like(wsig)

    for r, d in enumerate(rounds):

        @pl.when(me < d)
        def _():
            got[r, :, :hd, :] = jnp.zeros((elecs, hd, INNER), BF16)
            got[r, :, hd:, :] = jnp.ones((elecs, 16, INNER), BF16)

    wd[...] = jnp.zeros_like(wd)
    wd[:, :HEADS] = wdec_ref[...].astype(F32)

    def piece(slot, src, i, peer):
        span = pl.ds(i * per, per)
        return pltpu.make_async_remote_copy(
            src_ref=src.at[:, span, :],
            dst_ref=esig.at[slot, :, span, :],
            send_sem=esend.at[slot, i],
            recv_sem=erecv.at[slot, i],
            device_id={"elec": peer},
            device_id_type=MESH,
        )

    to_sib = [piece(0, sig, i, sib) for i in range(chunks)]
    to_far = [piece(1, sig, i, far) for i in range(chunks)]
    onward = [piece(2, esig.at[1], i, sib) for i in range(chunks)]
    to_next = [
        pltpu.make_async_remote_copy(
            src_ref=sig.at[e],
            dst_ref=wsig.at[e],
            send_sem=wsend.at[e],
            recv_sem=wrecv.at[e],
            device_id={"tm": me + 1},
            device_id_type=MESH,
        )
        for e in range(elecs)
    ]
    states = [
        pltpu.make_async_remote_copy(
            src_ref=msg.at[r],
            dst_ref=got.at[r],
            send_sem=ssend.at[r],
            recv_sem=srecv.at[r],
            device_id={"tm": me + d},
            device_id_type=MESH,
        )
        for r, d in enumerate(rounds)
    ]

    local[0].wait()
    pl.semaphore_wait(barrier, targets)
    for i in range(chunks):
        to_far[i].start()

    @pl.when(me + 1 < n_tm)
    def _():
        for copy in to_next:
            copy.start()

    for i in range(chunks):
        to_sib[i].start()
    local[1].wait()

    row = iota((times, INNER), 0)
    lane = iota((times, INNER), 1)
    causal = row >= lane
    lane_head = lane // hd
    flat = sig[...].reshape(elecs * times, width)
    logits_all = dot(flat, wd[...].astype(BF16))
    logits = logits_all[:times]
    for e in range(1, elecs):
        logits = logits + pltpu.roll(logits_all[e * times : (e + 1) * times], HEADS * e, 1)
    which = lax.rem(iota((1, INNER), 1), HEADS)
    rates = jnp.zeros((1, INNER), F32)
    for h in range(HEADS):
        rates = jnp.where(which == h, rate_ref[h], rates)
    soft = -2.0 * rates * jax.nn.sigmoid(logits)
    tri = jnp.where(causal, 1.0, 0.0)
    marks = jnp.where(causal, bound_ref[...].reshape(1, times).astype(F32), 0.0).astype(BF16)
    tri16 = tri.astype(BF16)
    soft_hi, soft_mid = split(soft)
    soft_lo = (soft - soft_hi.astype(F32) - soft_mid.astype(F32)).astype(BF16)
    bounds = dot(marks, jnp.ones((times, INNER), BF16))
    cum = dot(tri16, soft_hi) + dot(tri16, soft_mid) + dot(tri16, soft_lo) + math.log(0.5) * bounds
    cum2 = cum * LOG2E
    cum2_t = cum2.T
    proj[:, :, :384] = dot(flat, wqkv[:, :384]).astype(BF16).reshape(elecs, times, 384)

    block_diag = (row // hd) == lane_head
    inc_state, inc_dec = [], []
    for e in range(elecs):
        spread = jnp.broadcast_to(cum2[:, HEADS * e : HEADS * e + 1], (times, INNER))
        for h in range(1, HEADS):
            at = HEADS * e + h
            spread = jnp.where(
                lane_head == h, jnp.broadcast_to(cum2[:, at : at + 1], (times, INNER)), spread
            )
        cum_lanes[e] = spread
        ending = spread[times - 1 : times, :]
        kept = jnp.exp2(ending - spread)
        high, low = split((proj[e, :, 128:256].astype(F32) * kept).T)
        values = proj[e, :, 256:384]
        full = jnp.where(block_diag, dot(high, values) + dot(low, values), 0.0)
        small = full[:hd]
        for h in range(1, HEADS):
            small = small + full[h * hd : (h + 1) * hd]
        inc_state.append(small)
        inc_dec.append(jnp.exp2(ending))
    exc_state = [jnp.zeros((hd, INNER), F32)] * elecs
    exc_dec = [jnp.ones((1, INNER), F32)] * elecs

    def send_states(r, d):
        for e in range(elecs):
            msg[r, e, :hd, :] = inc_state[e].astype(BF16)
            msg[r, e, hd:, :] = jnp.broadcast_to(inc_dec[e], (16, INNER)).astype(BF16)

        @pl.when(me + d < n_tm)
        def _():
            states[r].start()

    def take_states(r, d):
        @pl.when(me >= d)
        def _():
            states[r].wait_recv()

        for e in range(elecs):
            came = got[r, e, :hd, :].astype(F32)
            dec = got[r, e, hd:, :].astype(F32)[:1]
            exc_state[e] = exc_dec[e] * came + exc_state[e]
            exc_dec[e] = exc_dec[e] * dec
            inc_state[e] = inc_dec[e] * came + inc_state[e]
            inc_dec[e] = inc_dec[e] * dec
        if r + 1 < len(rounds):
            send_states(r + 1, rounds[r + 1])

    send_states(0, rounds[0])

    proj[:, :, 384:768] = dot(flat, wqkv[:, 384:768]).astype(BF16).reshape(elecs, times, 384)
    own = dot(flat, wqkv[:, 768:1152]).astype(BF16).astype(F32).reshape(elecs, times, 384)
    eq[...] = own[:, :, :128]
    ekv[...] = own[:, :, 128:]

    head_row = iota((1, INNER), 1) // hd
    head_masks = [jnp.where(head_row == h, 1.0, 0.0) for h in range(HEADS)]
    masks16 = [m.astype(BF16) for m in head_masks]

    def by_head(query):
        return jnp.concatenate([query * m for m in masks16], axis=0)

    def pick(stacked, rows):
        head = iota((rows, INNER), 1) // hd
        result = stacked[:rows]
        for h in range(1, HEADS):
            result = jnp.where(head == h, stacked[h * rows : (h + 1) * rows], result)
        return result

    def linear(e):
        scores = dot_t(by_head(proj[e, :, :128]), proj[e, :, 128:256])
        weights = []
        for h in range(HEADS):
            at = HEADS * e + h
            gap = cum2[:, at : at + 1] - cum2_t[at : at + 1, :]
            decays = jnp.exp2(jnp.where(causal, gap, -jnp.inf))
            weights.append((scores[h * times : (h + 1) * times] * scale * decays).astype(BF16))
        raw[e] = pick(dot(jnp.concatenate(weights, axis=0), proj[e, :, 256:384]), times)

    fold = scale * LOG2E
    neg = -jnp.inf
    ones_keys = jnp.ones((2 * times, INNER), BF16)

    def window(e):
        @pl.when(me >= 1)
        def _():
            to_next[e].wait_recv()

        prior = dot(wsig[e], wqkv[:, 512:768]).astype(BF16)
        keys = jnp.concatenate([prior[:, :128], proj[e, :, 512:640]], axis=0)
        values = jnp.concatenate([prior[:, 128:], proj[e, :, 640:768]], axis=0)
        scores = dot_t(by_head(proj[e, :, 384:512]), keys)
        before = (lane >= row) & (me > 0)
        weights = []
        for h in range(HEADS):
            part = scores[h * times : (h + 1) * times]
            old = jnp.where(before, part[:, :times], neg)
            new = jnp.where(causal, part[:, times:], neg)
            peak = jnp.max(jnp.maximum(old, new), axis=1, keepdims=True)
            weights.append(
                jnp.concatenate(
                    [
                        jnp.exp2((old - peak) * fold).astype(BF16),
                        jnp.exp2((new - peak) * fold).astype(BF16),
                    ],
                    axis=1,
                )
            )
        both = dot(
            jnp.concatenate(weights, axis=0), jnp.concatenate([values, ones_keys], axis=1)
        )
        return pick(both[:, :128], times) / pick(both[:, 128:], times)

    qrows = elecs * GROUP
    krows = 4 * elecs * GROUP
    erow = iota((HEADS * qrows, krows), 0)
    ecol = iota((HEADS * qrows, krows), 1)
    good = jnp.zeros((1, krows), jnp.int32)
    col_elec = iota((1, krows), 1) // GROUP
    for slot, peer in enumerate((who, sib, far, far_sib)):
        for i in range(elecs):
            good = jnp.where(col_elec == slot * elecs + i, valid_ref[peer * elecs + i], good)
    eallowed = (lax.rem(erow, GROUP) == lax.rem(ecol, GROUP)) & (
        (jnp.broadcast_to(good, ecol.shape) == 1)
        | (ecol // GROUP == lax.rem(erow // GROUP, elecs))
    )
    ones_ele = jnp.ones((krows, INNER), BF16)

    def electrode(i):
        span = pl.ds(i * per, per)
        there = esig[:, :, span, :].reshape(3 * elecs * per, width)
        kv = dot(there, wqkv[:, 896:1152]).astype(BF16).astype(F32)
        kv = kv.reshape(3 * elecs, per, 256)
        for g in range(per // GROUP):
            begin = i * per + g * GROUP
            mine = ekv[:, begin : begin + GROUP, :].reshape(qrows, 256)
            rest = kv[:, g * GROUP : (g + 1) * GROUP, :].reshape(krows - qrows, 256)
            pair = jnp.concatenate([mine, rest], axis=0).astype(BF16)
            query = eq[:, begin : begin + GROUP, :].reshape(qrows, 128).astype(BF16)
            scores = jnp.where(eallowed, dot_t(by_head(query), pair[:, :128]), neg)
            peak = jnp.max(scores, axis=1, keepdims=True)
            weights = jnp.exp2((scores - peak) * fold).astype(BF16)
            both = dot(weights, jnp.concatenate([pair[:, 128:], ones_ele], axis=1))
            result = pick(both[:, :128], qrows) / pick(both[:, 128:], qrows)
            ele[:, begin : begin + GROUP, :] = result.reshape(elecs, GROUP, INNER)

    def forward(i):
        to_far[i].wait_recv()
        onward[i].start()

    linear(0)
    linear(1)
    take_states(0, rounds[0])
    linear(2)
    linear(3)
    forward(0)
    if len(rounds) > 1:
        take_states(1, rounds[1])
    win = [window(0)]
    forward(1)
    to_sib[0].wait_recv()
    onward[0].wait_recv()
    electrode(0)
    if len(rounds) > 2:
        take_states(2, rounds[2])
    win.append(window(1))
    forward(2)
    to_sib[1].wait_recv()
    onward[1].wait_recv()
    electrode(1)
    win.append(window(2))
    forward(3)
    to_sib[2].wait_recv()
    onward[2].wait_recv()
    electrode(2)
    win.append(window(3))
    for r in range(3, len(rounds)):
        take_states(r, rounds[r])
    gain = gain_ref[...].reshape(1, INNER)
    lin = []
    for e in range(elecs):
        tiled = jnp.concatenate([exc_state[e]] * HEADS, axis=0)
        s_hi, s_lo = split(jnp.where(block_diag, tiled, 0.0))
        q_hi, q_lo = split(proj[e, :, :128].astype(F32) * (jnp.exp2(cum_lanes[e]) * scale))
        total = raw[e] + dot(q_hi, s_hi) + dot(q_hi, s_lo) + dot(q_lo, s_hi)
        square = jnp.mean(total * total, axis=1, keepdims=True)
        lin.append((total * lax.rsqrt(square + 1e-05) * gain).astype(BF16))
    to_sib[3].wait_recv()
    onward[3].wait_recv()
    electrode(3)
    local[2].wait()
    for e in range(elecs):
        mixed = jnp.concatenate([lin[e], win[e].astype(BF16), ele[e].astype(BF16)], axis=1)
        out_ref[e] = (sig[e].astype(F32) + dot(mixed, wout[...])).astype(BF16)

    for copy in to_sib + to_far + onward:
        copy.wait_send()

    @pl.when(me + 1 < n_tm)
    def _():
        for copy in to_next:
            copy.wait_send()

    for r, d in enumerate(rounds):

        @pl.when(me + d < n_tm)
        def _():
            states[r].wait_send()


def shards(n_tm, signal, w_qkv, w_decay, decay_rate, lin_gain, w_out, valid, boundary):
    elecs, times, width = signal.shape
    hd = INNER // HEADS
    rounds = max(1, (n_tm - 1).bit_length())
    chunks = 4
    anywhere = pl.BlockSpec(memory_space=pl.ANY)
    vmem = pl.BlockSpec(memory_space=pltpu.VMEM)
    smem = pl.BlockSpec(memory_space=pltpu.SMEM)
    dma = pltpu.SemaphoreType.DMA
    return pl.pallas_call(
        functools.partial(kernel, n_tm, chunks),
        out_shape=jax.ShapeDtypeStruct(signal.shape, BF16),
        in_specs=[anywhere, anywhere, vmem, smem, vmem, anywhere, smem, vmem],
        out_specs=vmem,
        scratch_shapes=[
            pltpu.VMEM(signal.shape, BF16),
            pltpu.VMEM(w_qkv.shape, BF16),
            pltpu.VMEM(w_out.shape, BF16),
            pltpu.VMEM((width, INNER), F32),
            pltpu.VMEM((3, elecs, times, width), BF16),
            pltpu.VMEM((elecs, times, width), BF16),
            pltpu.VMEM((elecs, times, 768), BF16),
            pltpu.VMEM((elecs, times, 256), F32),
            pltpu.VMEM((elecs, times, INNER), F32),
            pltpu.VMEM((elecs, times, INNER), F32),
            pltpu.VMEM((elecs, times, INNER), F32),
            pltpu.VMEM((elecs, times, INNER), F32),
            pltpu.VMEM((rounds, elecs, hd + 16, INNER), BF16),
            pltpu.VMEM((rounds, elecs, hd + 16, INNER), BF16),
            dma((3,)),
            dma((3, chunks)),
            dma((3, chunks)),
            dma((elecs,)),
            dma((elecs,)),
            dma((rounds,)),
            dma((rounds,)),
        ],
        compiler_params=pltpu.CompilerParams(
            collective_id=0, has_side_effects=True, vmem_limit_bytes=48 * 2**20
        ),
    )(signal, w_qkv, w_decay, decay_rate, lin_gain, w_out, valid, boundary)


def solution(mesh):
    return jax.shard_map(
        functools.partial(shards, mesh.shape["tm"]),
        mesh=mesh,
        in_specs=(P("elec", "tm", None), P(), P(), P(), P(), P(), P(), P("tm")),
        out_specs=P("elec", "tm", None),
        check_vma=False,
    )
```

time: 120 us -> 27.4 us (0.23)
  the two profiles are of different devices: /device:TPU:0 before, /device:TPU:24 now
where the time goes in v1:
time: 27.4 us; the launch traced here: 27.2 us
  Pallas kernels  22.6 us (82%)
  local copies, waits for them, and re-layouts  4.52 us (16%)
    pallas_call x1, Pallas kernels, shards(): pl.pallas_call(functools.partial(kernel, n_tm, chunks), out_shape=jax.Sha...  22.6 us
    unnamed x16, local copies, waits for them, and re-layouts  4.52 us

profile of v1, /device:TPU:24, one launch (start us, length us, event | category | flops | bytes accessed | tf_op | source)
XLA Modules:
  0.0 27.2 jit_solution(460469663072988695)
XLA Ops:
  0.0 0.0 copy-start.6
  0.0 0.0 copy-start.5
  0.0 0.0 copy-start.4
  0.0 0.0 copy-start.3
  0.0 0.9 %copy.9.wdec_ref = bf16[256,4]{1,0:T(8,128)(2,1)S(1)} copy(bf16[256,4]{0,1:T(4,128)(2,1)} %param.10) | data formatting | bytes 4096 | tf_op args[2]
  0.9 0.0 copy-done.6
  0.9 0.0 copy-done.5
  0.9 0.0 copy-done.4
  0.9 0.0 copy-done.3
  0.9 0.0 copy-start
  0.9 1.1 %copy-done = bf16[256,1152]{1,0:T(8,128)(2,1)S(1)} copy-done((bf16[256,1152]{1,0:T(8,128)(2,1)S(1)}, bf16[256,1152]{1,0:T(8,128)(2,1)}, u32[]{:S(2)}) %copy-start) | copy-done | bytes 589848
  2.0 0.0 copy-start.1
  2.0 0.9 %copy-done.1 = bf16[4,128,256]{2,1,0:T(8,128)(2,1)S(1)} copy-done((bf16[4,128,256]{2,1,0:T(8,128)(2,1)S(1)}, bf16[4,128,256]{2,1,0:T(8,128)(2,1)}, u32[]{:S(2)}) %copy-start.1) | copy-done | bytes 262168
  2.9 0.0 copy-start.2
  2.9 0.9 %copy-done.2 = bf16[384,256]{1,0:T(8,128)(2,1)S(1)} copy-done((bf16[384,256]{1,0:T(8,128)(2,1)S(1)}, bf16[384,256]{1,0:T(8,128)(2,1)}, u32[]{:S(2)}) %copy-start.2) | copy-done | bytes 196632
  3.9 22.6 %shard_map.82 = bf16[4,128,256]{2,1,0:T(8,128)(2,1)S(1)} custom-call(bf16[4,128,256]{2,1,0:T(8,128)(2,1)S(1)} %copy-done.1, bf16[256,1152]{1,0:T(8,128)(2,1)S(1)} %copy-done, bf16[256,4]{1,0:T(8,128)(2,1)S(1)} %copy.9.wdec_ref, f32[4]{0:T(128)S(1)} %copy-done.3, f32[128]{0:T(128)S(1)} %copy-done.4, bf16[384,256]{1,0:T(8,128)(2,1)S(1)} %copy-done.2, ...), custom_call_target="tpu_custom_call" | custom-call | tf_op jit(solution)/shard_map/pallas_call | solution.py:412
  26.5 0.7 %copy.11 = bf16[4,128,256]{2,1,0:T(8,128)(2,1)} copy(bf16[4,128,256]{2,1,0:T(8,128)(2,1)S(1)} %shard_map.82) | data formatting | bytes 524288
Async XLA Ops:
  0.0 0.9 %copy-start.6 = (s32[128]{0:T(128)S(1)}, s32[128]{0:T(128)}, u32[]{:S(2)}) copy-start(s32[128]{0:T(128)} %bound_ref.1) | copy-start | bytes 1540
  0.0 0.9 %copy-start.5 = (s32[16]{0:T(128)S(1)}, s32[16]{0:T(128)}, u32[]{:S(2)}) copy-start(s32[16]{0:T(128)} %valid_ref.1) | copy-start | bytes 196
  0.0 0.9 %copy-start.4 = (f32[128]{0:T(128)S(1)}, f32[128]{0:T(128)}, u32[]{:S(2)}) copy-start(f32[128]{0:T(128)} %gain_ref.1) | copy-start | bytes 1540
  0.0 0.9 %copy-start.3 = (f32[4]{0:T(128)S(1)}, f32[4]{0:T(128)}, u32[]{:S(2)}) copy-start(f32[4]{0:T(128)} %rate_ref.1) | copy-start | bytes 52
  0.9 1.1 %copy-start = (bf16[256,1152]{1,0:T(8,128)(2,1)S(1)}, bf16[256,1152]{1,0:T(8,128)(2,1)}, u32[]{:S(2)}) copy-start(bf16[256,1152]{1,0:T(8,128)(2,1)} %wqkv_in.1) | copy-start | bytes 1769476
  2.0 0.9 %copy-start.1 = (bf16[4,128,256]{2,1,0:T(8,128)(2,1)S(1)}, bf16[4,128,256]{2,1,0:T(8,128)(2,1)}, u32[]{:S(2)}) copy-start(bf16[4,128,256]{2,1,0:T(8,128)(2,1)} %sig_in.1) | copy-start | bytes 786436
  2.9 0.9 %copy-start.2 = (bf16[384,256]{1,0:T(8,128)(2,1)S(1)}, bf16[384,256]{1,0:T(8,128)(2,1)}, u32[]{:S(2)}) copy-start(bf16[384,256]{1,0:T(8,128)(2,1)} %wout_in.1) | copy-start | bytes 589828

commit v2 on v1

--- a/solution.py
+++ b/solution.py
@@ -16,6 +16,7 @@
 BF16 = jnp.bfloat16
 MESH = pl.DeviceIdType.MESH
 GROUP = 8
+EARLY = 1
 
 
 def dot(a, b):
@@ -40,16 +41,21 @@
     chunks,
     sig_in,
     wqkv_in,
-    wdec_ref,
-    rate_ref,
-    gain_ref,
+    wdec_in,
+    rate_in,
+    gain_in,
     wout_in,
-    valid_ref,
-    bound_ref,
+    valid_in,
+    bound_in,
     out_ref,
     sig,
     wqkv,
     wout,
+    wdec_ref,
+    rate_ref,
+    gain_ref,
+    valid_ref,
+    bound_ref,
     wd,
     esig,
     wsig,
@@ -86,7 +92,18 @@
 
     local = [
         pltpu.make_async_copy(src, dst, local_sem.at[i])
-        for i, (src, dst) in enumerate(((sig_in, sig), (wqkv_in, wqkv), (wout_in, wout)))
+        for i, (src, dst) in enumerate(
+            (
+                (sig_in, sig),
+                (wqkv_in, wqkv),
+                (wout_in, wout),
+                (wdec_in, wdec_ref),
+                (rate_in, rate_ref),
+                (gain_in, gain_ref),
+                (valid_in, valid_ref),
+                (bound_in, bound_ref),
+            )
+        )
     ]
     for copy in local:
         copy.start()
@@ -109,11 +126,10 @@
 
         @pl.when(me < d)
         def _():
-            got[r, :, :hd, :] = jnp.zeros((elecs, hd, INNER), BF16)
-            got[r, :, hd:, :] = jnp.ones((elecs, 16, INNER), BF16)
+            got[r, : elecs * hd, :] = jnp.zeros((elecs * hd, INNER), BF16)
+            got[r, elecs * hd :, :] = jnp.ones((16, INNER), BF16)
 
     wd[...] = jnp.zeros_like(wd)
-    wd[:, :HEADS] = wdec_ref[...].astype(F32)
 
     def piece(slot, src, i, peer):
         span = pl.ds(i * per, per)
@@ -152,26 +168,16 @@
         for r, d in enumerate(rounds)
     ]
 
-    local[0].wait()
-    pl.semaphore_wait(barrier, targets)
-    for i in range(chunks):
-        to_far[i].start()
-
-    @pl.when(me + 1 < n_tm)
-    def _():
-        for copy in to_next:
-            copy.start()
-
-    for i in range(chunks):
-        to_sib[i].start()
-    local[1].wait()
+    for i in (0, 3, 4, 5, 6, 7):
+        local[i].wait()
+    wd[:HEADS, :] = wdec_ref[...].astype(F32)
 
     row = iota((times, INNER), 0)
     lane = iota((times, INNER), 1)
     causal = row >= lane
     lane_head = lane // hd
     flat = sig[...].reshape(elecs * times, width)
-    logits_all = dot(flat, wd[...].astype(BF16))
+    logits_all = dot_t(flat, wd[...].astype(BF16))
     logits = logits_all[:times]
     for e in range(1, elecs):
         logits = logits + pltpu.roll(logits_all[e * times : (e + 1) * times], HEADS * e, 1)
@@ -189,6 +195,20 @@
     cum = dot(tri16, soft_hi) + dot(tri16, soft_mid) + dot(tri16, soft_lo) + math.log(0.5) * bounds
     cum2 = cum * LOG2E
     cum2_t = cum2.T
+    pl.semaphore_wait(barrier, targets)
+    for i in range(chunks):
+        to_far[i].start()
+    for i in range(chunks):
+        to_sib[i].start()
+
+    def send_window(first, last):
+        @pl.when(me + 1 < n_tm)
+        def _():
+            for copy in to_next[first:last]:
+                copy.start()
+
+    send_window(0, EARLY)
+    local[1].wait()
     proj[:, :, :384] = dot(flat, wqkv[:, :384]).astype(BF16).reshape(elecs, times, 384)
 
     block_diag = (row // hd) == lane_head
@@ -216,8 +236,11 @@
 
     def send_states(r, d):
         for e in range(elecs):
-            msg[r, e, :hd, :] = inc_state[e].astype(BF16)
-            msg[r, e, hd:, :] = jnp.broadcast_to(inc_dec[e], (16, INNER)).astype(BF16)
+            msg[r, e * hd : (e + 1) * hd, :] = inc_state[e].astype(BF16)
+        packed = jnp.broadcast_to(inc_dec[0], (16, INNER))
+        for e in range(1, elecs):
+            packed = jnp.where(iota((16, INNER), 0) == e, inc_dec[e], packed)
+        msg[r, elecs * hd :, :] = packed.astype(BF16)
 
         @pl.when(me + d < n_tm)
         def _():
@@ -228,9 +251,10 @@
         def _():
             states[r].wait_recv()
 
+        decs = got[r, elecs * hd :, :].astype(F32)
         for e in range(elecs):
-            came = got[r, e, :hd, :].astype(F32)
-            dec = got[r, e, hd:, :].astype(F32)[:1]
+            came = got[r, e * hd : (e + 1) * hd, :].astype(F32)
+            dec = decs[e : e + 1]
             exc_state[e] = exc_dec[e] * came + exc_state[e]
             exc_dec[e] = exc_dec[e] * dec
             inc_state[e] = inc_dec[e] * came + inc_state[e]
@@ -239,6 +263,7 @@
             send_states(r + 1, rounds[r + 1])
 
     send_states(0, rounds[0])
+    send_window(EARLY, elecs)
 
     proj[:, :, 384:768] = dot(flat, wqkv[:, 384:768]).astype(BF16).reshape(elecs, times, 384)
     own = dot(flat, wqkv[:, 768:1152]).astype(BF16).astype(F32).reshape(elecs, times, 384)
@@ -340,33 +365,31 @@
         to_far[i].wait_recv()
         onward[i].start()
 
+    def attend(i):
+        to_sib[i].wait_recv()
+        onward[i].wait_recv()
+        electrode(i)
+
+    win = []
     linear(0)
     linear(1)
+    forward(0)
+    linear(2)
+    forward(1)
+    linear(3)
     take_states(0, rounds[0])
-    linear(2)
-    linear(3)
-    forward(0)
+    win.append(window(0))
+    attend(0)
+    forward(2)
     if len(rounds) > 1:
         take_states(1, rounds[1])
-    win = [window(0)]
-    forward(1)
-    to_sib[0].wait_recv()
-    onward[0].wait_recv()
-    electrode(0)
-    if len(rounds) > 2:
-        take_states(2, rounds[2])
     win.append(window(1))
-    forward(2)
-    to_sib[1].wait_recv()
-    onward[1].wait_recv()
-    electrode(1)
+    attend(1)
+    forward(3)
     win.append(window(2))
-    forward(3)
-    to_sib[2].wait_recv()
-    onward[2].wait_recv()
-    electrode(2)
+    attend(2)
     win.append(window(3))
-    for r in range(3, len(rounds)):
+    for r in range(2, len(rounds)):
         take_states(r, rounds[r])
     gain = gain_ref[...].reshape(1, INNER)
     lin = []
@@ -377,9 +400,7 @@
         total = raw[e] + dot(q_hi, s_hi) + dot(q_hi, s_lo) + dot(q_lo, s_hi)
         square = jnp.mean(total * total, axis=1, keepdims=True)
         lin.append((total * lax.rsqrt(square + 1e-05) * gain).astype(BF16))
-    to_sib[3].wait_recv()
-    onward[3].wait_recv()
-    electrode(3)
+    attend(3)
     local[2].wait()
     for e in range(elecs):
         mixed = jnp.concatenate([lin[e], win[e].astype(BF16), ele[e].astype(BF16)], axis=1)
@@ -405,20 +426,23 @@
     hd = INNER // HEADS
     rounds = max(1, (n_tm - 1).bit_length())
     chunks = 4
-    anywhere = pl.BlockSpec(memory_space=pl.ANY)
-    vmem = pl.BlockSpec(memory_space=pltpu.VMEM)
-    smem = pl.BlockSpec(memory_space=pltpu.SMEM)
+    hbm = pl.BlockSpec(memory_space=pltpu.HBM)
     dma = pltpu.SemaphoreType.DMA
     return pl.pallas_call(
         functools.partial(kernel, n_tm, chunks),
         out_shape=jax.ShapeDtypeStruct(signal.shape, BF16),
-        in_specs=[anywhere, anywhere, vmem, smem, vmem, anywhere, smem, vmem],
-        out_specs=vmem,
+        in_specs=[hbm] * 8,
+        out_specs=pl.BlockSpec(memory_space=pltpu.VMEM),
         scratch_shapes=[
             pltpu.VMEM(signal.shape, BF16),
             pltpu.VMEM(w_qkv.shape, BF16),
             pltpu.VMEM(w_out.shape, BF16),
-            pltpu.VMEM((width, INNER), F32),
+            pltpu.VMEM((HEADS, width), BF16),
+            pltpu.SMEM(decay_rate.shape, F32),
+            pltpu.VMEM(lin_gain.shape, F32),
+            pltpu.SMEM(valid.shape, jnp.int32),
+            pltpu.VMEM(boundary.shape, jnp.int32),
+            pltpu.VMEM((INNER, width), F32),
             pltpu.VMEM((3, elecs, times, width), BF16),
             pltpu.VMEM((elecs, times, width), BF16),
             pltpu.VMEM((elecs, times, 768), BF16),
@@ -427,9 +451,9 @@
             pltpu.VMEM((elecs, times, INNER), F32),
             pltpu.VMEM((elecs, times, INNER), F32),
             pltpu.VMEM((elecs, times, INNER), F32),
-            pltpu.VMEM((rounds, elecs, hd + 16, INNER), BF16),
-            pltpu.VMEM((rounds, elecs, hd + 16, INNER), BF16),
-            dma((3,)),
+            pltpu.VMEM((rounds, elecs * hd + 16, INNER), BF16),
+            pltpu.VMEM((rounds, elecs * hd + 16, INNER), BF16),
+            dma((8,)),
             dma((3, chunks)),
             dma((3, chunks)),
             dma((elecs,)),
@@ -438,9 +462,9 @@
             dma((rounds,)),
         ],
         compiler_params=pltpu.CompilerParams(
-            collective_id=0, has_side_effects=True, vmem_limit_bytes=48 * 2**20
+            collective_id=0, has_side_effects=True
         ),
-    )(signal, w_qkv, w_decay, decay_rate, lin_gain, w_out, valid, boundary)
+    )(signal, w_qkv, w_decay.T, decay_rate, lin_gain, w_out, valid, boundary)
 
 
 def solution(mesh):

time: 27.4 us -> 20.5 us (0.75)
  the two profiles are of different devices: /device:TPU:24 before, /device:TPU:0 now
where the time goes in v2:
time: 20.5 us; the launch traced here: 20.4 us
  Pallas kernels  18.7 us (91%)
  local copies, waits for them, and re-layouts  1.67 us (8%)
    pallas_call x1, Pallas kernels, shards(): pl.pallas_call(functools.partial(kernel, n_tm, chunks), out_shape=jax.Sha...  18.7 us
    unnamed x1, local copies, waits for them, and re-layouts  1.67 us

profile of v2, /device:TPU:0, one launch (start us, length us, event | category | flops | bytes accessed | tf_op | source)
XLA Modules:
  0.0 20.4 jit_solution(27553068201445037)
XLA Ops:
  0.0 18.7 %shard_map.82 = bf16[4,128,256]{2,1,0:T(8,128)(2,1)} custom-call(bf16[4,128,256]{2,1,0:T(8,128)(2,1)} %sig_in.1, bf16[256,1152]{1,0:T(8,128)(2,1)} %wqkv_in.1, bf16[4,256]{1,0:T(4,128)(2,1)} %bitcast.1, f32[4]{0:T(128)} %rate_in.1, f32[128]{0:T(128)} %gain_in.1, bf16[384,256]{1,0:T(8,128)(2,1)} %wout_in.1, s32[16]{0:T(128)} %valid_in.1, s32[128]{0:T(128)} %bound_in.1), custom_call_target="tpu_custom_call" | custom-call | tf_op jit(solution)/shard_map/pallas_call | solution.py:431
  18.7 1.7 %copy.10 = bf16[4,128,256]{2,1,0:T(8,128)(2,1)} copy(bf16[4,128,256]{2,1,0:T(8,128)(2,1)} %shard_map.82) | data formatting | bytes 524288

commit v3 on v2

--- a/solution.py
+++ b/solution.py
@@ -375,8 +375,8 @@
     linear(1)
     forward(0)
     linear(2)
+    linear(3)
     forward(1)
-    linear(3)
     take_states(0, rounds[0])
     win.append(window(0))
     attend(0)
@@ -384,8 +384,8 @@
     if len(rounds) > 1:
         take_states(1, rounds[1])
     win.append(window(1))
+    forward(3)
     attend(1)
-    forward(3)
     win.append(window(2))
     attend(2)
     win.append(window(3))

time: 20.5 us -> 20.2 us (0.985)
  Pallas kernels: 18.7 us -> 18.4 us
    pallas_call x1, Pallas kernels: 18.7 us -> 18.4 us  [shards(): pl.pallas_call(functools.partial(kernel, n_tm, chunks), out_shape=jax.Sha...]
where the time goes in v3:
time: 20.2 us; the launch traced here: 20 us
  Pallas kernels  18.4 us (91%)
  local copies, waits for them, and re-layouts  1.67 us (8%)
    pallas_call x1, Pallas kernels, shards(): pl.pallas_call(functools.partial(kernel, n_tm, chunks), out_shape=jax.Sha...  18.4 us
    unnamed x1, local copies, waits for them, and re-layouts  1.67 us

profile of v3, /device:TPU:0, one launch (start us, length us, event | category | flops | bytes accessed | tf_op | source)
XLA Modules:
  0.0 20.0 jit_solution(18426094780624551519)
XLA Ops:
  0.0 18.4 %shard_map.82 = bf16[4,128,256]{2,1,0:T(8,128)(2,1)} custom-call(bf16[4,128,256]{2,1,0:T(8,128)(2,1)} %sig_in.1, bf16[256,1152]{1,0:T(8,128)(2,1)} %wqkv_in.1, bf16[4,256]{1,0:T(4,128)(2,1)} %bitcast.1, f32[4]{0:T(128)} %rate_in.1, f32[128]{0:T(128)} %gain_in.1, bf16[384,256]{1,0:T(8,128)(2,1)} %wout_in.1, s32[16]{0:T(128)} %valid_in.1, s32[128]{0:T(128)} %bound_in.1), custom_call_target="tpu_custom_call" | custom-call | tf_op jit(solution)/shard_map/pallas_call | solution.py:431
  18.4 1.7 %copy.10 = bf16[4,128,256]{2,1,0:T(8,128)(2,1)} copy(bf16[4,128,256]{2,1,0:T(8,128)(2,1)} %shard_map.82) | data formatting | bytes 524288
